TPU v7x, 32 devices: a whole 2x2x4 slice. The times are simulated.
32 devices in a mesh: view: 8 (over y, x, core), walk: 4 (over z).
Axes of the slice: x: 2, y: 2, z: 4, core: 2. Of those that a mesh axis runs over, the one named last changes fastest.
Arguments:
- positions: float32 [64, 1024], P('walk', 'view'), may hold values from -21 to 21
- tile_values: bfloat16 [512, 128, 128], P('view'), may hold values from -0.25 to 0.25
- tile_rays: int32 [512], P('view'), may hold values from 0 to 15, as said below
- tile_voxels: int32 [512], P('view'), may hold values from 0 to 7
- tile_count: int32 [8], P('view'), may hold values from 16 to 64, as said below
- measured: float32 [16384], P('view'), may hold values from -6 to 6
- langevin_noise: float32 [64, 64], P('walk'), may hold values from -6 to 6
Outputs:
- gradient: float32 [64, 1024], P('walk', 'view')
- displacement: float32 [64, 1024], P('walk', 'view')
Inputs may be any that keep to these rules, and one draw needn't show every extreme that they name: `tile_rays`: the 64 slots of one view index name distinct pairs of ray block and voxel block, live slots or not. The live slots of a view index are its first tile_count slots; some view index has all 64 live.
All inputs are finite; a program needn't handle non-finite values.
Results may differ from a plain program's by a relative error of at most 0.0029.
Values may be sent and summed in bfloat16 or wider, within the bound.
A program may use at most 64 MiB of HBM per device.

v0:
```python
import math

import jax
import jax.numpy as jnp
from jax import lax
from jax.sharding import PartitionSpec as P

misfit_weight = 4.0


def forward_kernel(blocks, ray_blocks):

    def kernel(values, ray_ids, vox_ids, live_mask):
        picked = jnp.take(blocks, vox_ids, axis=1)
        product = jnp.einsum("gri,jgi->gjr", values, picked, preferred_element_type=jnp.float32)
        select = (
            (ray_ids[None, :] == jnp.arange(ray_blocks, dtype=jnp.int32)[:, None])
            & live_mask[None, :]
        ).astype(jnp.float32)
        return jnp.einsum("bg,gjr->jbr", select, product, precision=lax.Precision.HIGHEST)

    return kernel


def adjoint_kernel(residual_blocks, voxel_blocks):

    def kernel(values, ray_ids, vox_ids, live_mask):
        picked = jnp.take(residual_blocks, ray_ids, axis=1)
        product = jnp.einsum("gri,jgr->gji", values, picked, preferred_element_type=jnp.float32)
        select = (
            (vox_ids[None, :] == jnp.arange(voxel_blocks, dtype=jnp.int32)[:, None])
            & live_mask[None, :]
        ).astype(jnp.float32)
        return jnp.einsum("bg,gji->jbi", select, product, precision=lax.Precision.HIGHEST)

    return kernel


def sweep(kernel, values, ray_ids, vox_ids, live_count):
    slot_count = values.shape[0]
    live_mask = jnp.arange(slot_count, dtype=jnp.int32) < live_count
    return kernel(values, ray_ids, vox_ids, live_mask)


def shards(positions, tile_values, tile_rays, tile_voxels, tile_count, measured, langevin_noise):
    local_walkers, local_voxels = positions.shape
    tile_size = tile_values.shape[1]
    ensemble = lax.all_gather(positions, "walk", axis=0, tiled=True)
    volume = lax.all_gather(positions.astype(jnp.bfloat16), "view", axis=1, tiled=True)
    voxel_count = volume.shape[1]
    voxel_blocks = voxel_count // tile_size
    ray_blocks = measured.shape[0] // tile_size
    blocks = volume.reshape(local_walkers, voxel_blocks, tile_size)
    live_count = tile_count[0]
    projected = sweep(
        forward_kernel(blocks, ray_blocks), tile_values, tile_rays, tile_voxels, live_count
    )
    residual = (projected - measured.reshape(ray_blocks, tile_size)[None, :, :]).astype(
        jnp.bfloat16
    )
    partial_back = sweep(
        adjoint_kernel(residual, voxel_blocks), tile_values, tile_rays, tile_voxels, live_count
    )
    partial_back = partial_back.reshape(local_walkers, voxel_count)
    own_back = lax.psum_scatter(partial_back, "view", scatter_dimension=1, tiled=True)
    gradient = misfit_weight * own_back + positions
    walker_total = ensemble.shape[0]
    ensemble_mean = jnp.mean(ensemble, axis=0)
    deviation = ensemble - ensemble_mean[None, :]
    own_deviation = positions - ensemble_mean[None, :]
    gram_part = jnp.dot(deviation, gradient.T, precision=lax.Precision.HIGHEST)
    gram_matrix = lax.psum(gram_part, "view")
    step_size = walker_total / (4.0 * (voxel_count + 1))
    coefficient = (
        -(step_size / walker_total) * gram_matrix
        + math.sqrt(2.0 * step_size / walker_total) * langevin_noise.T
    )
    displacement = jnp.dot(coefficient.T, deviation, precision=lax.Precision.HIGHEST)
    displacement = displacement + step_size * (voxel_count + 1) / walker_total * own_deviation
    return (gradient, displacement)


def solution(mesh):
    in_specs = (
        P("walk", "view"),
        P("view", None, None),
        P("view"),
        P("view"),
        P("view"),
        P("view"),
        P("walk", None),
    )
    out_specs = (P("walk", "view"), P("walk", "view"))
    return jax.shard_map(shards, mesh=mesh, in_specs=in_specs, out_specs=out_specs, check_vma=False)
```

profile of v0, /device:TPU:0, one launch (start us, length us, event | category | flops | bytes accessed | tf_op | source)
XLA Modules:
  0.0 79.4 jit_solution(7303998576617407494)
XLA Ops:
  7.2 0.0 copy-start
  7.2 0.0 copy-start.5
  7.2 0.0 copy-start.3
  7.2 0.0 reduce-scatter.2.cloned.1.call-start
  7.2 0.8 %compare_select_fusion = s32[64]{0:T(128)S(1)} fusion(s32[64]{0:T(128)} %param.10), kind=kLoop, calls=%fused_computation.42 | loop fusion | flops 192 | bytes 512 | tf_op jit(solution)/shard_map/jit(_take)/jit(_where)/select_n | solution.py:14
  8.0 0.7 compare_and_fusion
  8.7 0.7 compare_select_fusion.1
  9.4 0.7 compare_and_fusion.1
  10.7 0.7 convert_element_type.8
  11.4 10.3 %all_gather.6 = bf16[16,1024]{1,0:T(8,128)(2,1)S(1)} all-gather(bf16[16,128]{1,0:T(8,128)(2,1)S(1)} %convert_element_type.8), channel_id=1, replica_groups=mesh['view'=8,'walk'=4] {'view'}, dimensions={1}, use_global_device_ids=true | all-gather | bytes 36864 | tf_op jit(solution)/shard_map/all_gather | solution.py:49
  21.7 0.6 gather_fusion
  22.4 0.0 copy-done
  22.4 1.2 %fusion.7 = f32[64,16,128]{2,1,0:T(8,128)S(1)} fusion(bf16[64,128,128]{2,1,0:T(8,128)(2,1)S(1)} %copy-done, bf16[64,16,128]{2,1,0:T(8,128)(2,1)S(1)} %gather_fusion, pred[64]{0:T(512)(128)(4,1)S(1)} %compare_and_fusion), kind=kOutput, calls=%fused_computation.11 | convolution fusion | flops 33685504 | bytes 2883648 | tf_op jit(solution)/shard_map/gri,jgi->gjr/dot_general | solution.py:15
  23.6 0.0 copy-start.6
  23.6 0.0 copy-done.5
  23.6 0.0 copy-done.3
  23.6 0.4 fusion.1
  24.1 0.0 copy-start.1
  24.1 0.0 copy-start.4
  24.1 0.6 gather_fusion.1
  24.8 0.7 fusion.5
  25.5 0.0 copy-done.6
  25.5 0.4 fusion.2
  25.9 0.6 copy.21
  26.5 0.0 reduce-scatter.2.cloned.1.call-update
  26.5 0.0 copy-done.1
  26.6 13.4 %all_gather.7 = f32[64,128]{1,0:T(8,128)S(1)} all-gather(f32[16,128]{1,0:T(8,128)S(1)} %copy-done.1), channel_id=1, replica_groups=mesh['view'=8,'walk'=4] {'walk'}, dimensions={0}, use_global_device_ids=true | all-gather | bytes 40960 | tf_op jit(solution)/shard_map/all_gather | solution.py:48
  39.9 18.5 %reduce-scatter.2.cloned.1.call-done = f32[16,128]{1,0:T(8,128)} async-done(((f32[16,1024]{1,0:T(8,128)}), f32[16,128]{1,0:T(8,128)}) %reduce-scatter.2.cloned.1.call-update) | async-done | bytes 8208 | tf_op jit(solution)/shard_map/reduce_scatter | solution.py:65
  58.4 0.7 multiply_add_fusion
  59.1 0.0 copy-start.2
  59.1 0.1 fusion.16
  59.3 12.5 %psum.7 = f32[64,16]{0,1:T(8,128)S(1)} all-reduce(f32[64,16]{0,1:T(8,128)S(1)} %fusion.16), channel_id=1, replica_groups=mesh['view'=8,'walk'=4] {'view'}, use_global_device_ids=true, to_apply=%region_2.3 | all-reduce | flops 1024 | bytes 8192 | tf_op jit(solution)/shard_map/psum | solution.py:72
  71.8 0.0 copy-done.4
  71.8 0.7 convolution_add_fusion
  72.5 0.0 copy-done.2
  (7 shorter events, 0.1 us)
Async XLA Ops:
  7.2 15.2 %copy-start = (bf16[64,128,128]{2,1,0:T(8,128)(2,1)S(1)}, bf16[64,128,128]{2,1,0:T(8,128)(2,1)}, u32[]{:S(2)}) copy-start(bf16[64,128,128]{2,1,0:T(8,128)(2,1)} %param.8) | copy-start | bytes 6291460
  7.2 16.4 %copy-start.5 = (s32[64]{0:T(128)S(1)}, s32[64]{0:T(128)}, u32[]{:S(2)}) copy-start(s32[64]{0:T(128)} %param.9) | copy-start | bytes 772
  7.2 16.4 %copy-start.3 = (f32[2048]{0:T(1024)S(1)}, f32[2048]{0:T(1024)}, u32[]{:S(2)}) copy-start(f32[2048]{0:T(1024)} %param.12) | copy-start | bytes 24580
  7.2 51.2 %reduce-scatter.2.cloned.1.call-start = ((), (), s32[]{:S(2)}) async-start(), calls=%async_computation.1 | async-start | bytes 73728 | tf_op jit(solution)/shard_map/reduce_scatter | solution.py:65
  23.6 1.9 %copy-start.6 = (s32[64]{0:T(128)S(1)}, s32[64]{0:T(128)}, u32[]{:S(2)}) copy-start(s32[64]{0:T(128)} %param.10) | copy-start | bytes 772
  24.1 2.5 %copy-start.1 = (f32[16,128]{1,0:T(8,128)S(1)}, f32[16,128]{1,0:T(8,128)}, u32[]{:S(2)}) copy-start(f32[16,128]{1,0:T(8,128)} %param.7) | copy-start | bytes 24580
  24.1 47.7 %copy-start.4 = (f32[16,64]{1,0:T(8,128)S(1)}, f32[16,64]{1,0:T(8,128)}, u32[]{:S(2)}) copy-start(f32[16,64]{1,0:T(8,128)} %param.13) | copy-start | bytes 12292
  59.1 13.4 %copy-start.2 = (f32[16,128]{1,0:T(8,128)}, f32[16,128]{1,0:T(8,128)S(1)}, u32[]{:S(2)}) copy-start(f32[16,128]{1,0:T(8,128)S(1)} %multiply_add_fusion) | copy-start | bytes 24580
Sparse Core Ops, SparseCore 0:
  26.7 31.6 reduce-scatter.1
where the time goes:
time: 79.7 us; the launch traced here: 79.4 us
  blocking collectives  36.2 us (45%)
  waiting for transfers between devices  18.5 us (23%)
  between operations  14.8 us (19%)
  other arithmetic  4.22 us (5%)
  matrix products  3.67 us (5%)
  local copies, waits for them, and re-layouts  1.97 us (2%)
    reduce_scatter x1, waiting for transfers between devices, shards(): lax.psum_scatter(partial_back, 'view', scatter_dimension=1, tiled=True)  18.5 us
    all_gather x1, blocking collectives, shards(): ensemble = lax.all_gather(positions, 'walk', axis=0, tiled=True)  13.4 us
    psum x1, blocking collectives, shards(): gram_matrix = lax.psum(gram_part, 'view')  12.5 us
    all_gather x1, blocking collectives, shards(): lax.all_gather(positions.astype(jnp.bfloat16), 'view', axis=1, tiled=True)  10.3 us
  transfers between devices with their start and end apart: 1, of which 1 were waited for; matrix products, arithmetic and copies ran while one was open for 0% of the time, Pallas kernels for 0%

commit v1 on v0

v1 whole, which is shorter than its diff:
```python
import functools
import math

import jax
import jax.numpy as jnp
from jax import lax
from jax.experimental import pallas as pl
from jax.experimental.pallas import tpu as pltpu
from jax.sharding import PartitionSpec as P

misfit_weight = 4.0
MESH = pl.DeviceIdType.MESH
GROUP = 8
CHUNKS = 4


def each(start, stop, body):
    if stop - start <= 16:
        for index in range(start, stop):
            body(index)
    else:

        @pl.loop(start, stop)
        def _(index):
            body(index)


def split_high_low(value):
    high = value.astype(jnp.bfloat16)
    low = (value - high.astype(jnp.float32)).astype(jnp.bfloat16)
    return high, low


def dot_t(left, right, precision=None):
    return lax.dot_general(
        left,
        right,
        (((1,), (1,)), ((), ())),
        precision=precision,
        preferred_element_type=jnp.float32,
    )


def step_kernel(
    views,
    walks,
    pos_ref,
    tiles_hbm,
    rays_ref,
    voxels_ref,
    count_ref,
    measured_ref,
    noise_ref,
    grad_ref,
    disp_ref,
    tiles,
    xpad,
    rpad,
    ens,
    devs,
    back,
    brecv,
    grecv,
    acc_f,
    tile_sem,
    x_send,
    x_recv,
    w_send,
    w_recv,
    d_send,
    d_recv,
    b_send,
    b_recv,
    g_send,
    g_recv,
):
    me_v = lax.axis_index("view")
    me_w = lax.axis_index("walk")
    rows = pos_ref.shape[0]
    slots, tile, _ = tiles.shape
    ray_blocks = measured_ref.shape[0]
    walkers = rows * walks
    voxel_count = views * tile
    chunk = slots // CHUNKS

    barrier = pltpu.get_barrier_semaphore()

    def greet_view(d):
        pl.semaphore_signal(
            barrier,
            inc=1,
            device_id={"view": lax.rem(me_v + d, views)},
            device_id_type=MESH,
        )

    def greet_walk(d):
        pl.semaphore_signal(
            barrier,
            inc=1,
            device_id={"walk": lax.rem(me_w + d, walks)},
            device_id_type=MESH,
        )

    each(1, walks, greet_walk)
    each(1, views, greet_view)

    def tile_copy(c):
        part = pl.ds(c * chunk, chunk)
        return pltpu.make_async_copy(tiles_hbm.at[part], tiles.at[part], tile_sem.at[c])

    for c in range(CHUNKS):
        tile_copy(c).start()

    positions = pos_ref[...]
    xpad[me_v, ray_blocks] = positions.astype(jnp.bfloat16)
    ens[me_w] = positions

    pl.semaphore_wait(barrier, views + walks - 2)

    def view_copy(d, src, dst, send, recv):
        return pltpu.make_async_remote_copy(
            src_ref=src,
            dst_ref=dst,
            send_sem=send.at[d],
            recv_sem=recv.at[d],
            device_id={"view": lax.rem(me_v + d, views)},
            device_id_type=MESH,
        )

    def origin(d):
        return lax.rem(me_v - d + views, views)

    def x_copy(d, owner):
        part = xpad.at[owner, ray_blocks]
        return view_copy(d, part, part, x_send, x_recv)

    def w_copy(d, owner):
        return pltpu.make_async_remote_copy(
            src_ref=ens.at[owner],
            dst_ref=ens.at[owner],
            send_sem=w_send.at[d],
            recv_sem=w_recv.at[d],
            device_id={"walk": lax.rem(me_w + d, walks)},
            device_id_type=MESH,
        )

    def d_copy(d, owner):
        return view_copy(d, devs.at[owner], devs.at[owner], d_send, d_recv)

    def b_copy(d, source, owner):
        return view_copy(d, back.at[source], brecv.at[owner], b_send, b_recv)

    def g_copy(d, owner):
        return view_copy(d, grecv.at[owner], grecv.at[owner], g_send, g_recv)

    each(1, views, lambda d: x_copy(d, me_v).start())
    each(1, walks, lambda d: w_copy(d, me_w).start())

    def clear(ref, index, middle):
        size = ref.shape[1]
        after = size - middle - 1
        ref[index, pl.ds(0, middle)] = jnp.zeros((middle, rows, tile), jnp.bfloat16)
        ref[index, pl.ds(middle + 1, after)] = jnp.zeros((after, rows, tile), jnp.bfloat16)

    each(0, views, lambda v: clear(xpad, v, ray_blocks))
    each(0, ray_blocks, lambda b: clear(rpad, b, views))

    each(1, walks, lambda d: w_copy(d, lax.rem(me_w - d + walks, walks)).wait_recv())
    ensemble = ens[...].reshape(walkers, tile)
    mean = jnp.sum(ensemble, axis=0, keepdims=True) / walkers
    deviation = ensemble - mean
    devs[me_v] = deviation.astype(jnp.bfloat16)
    each(1, views, lambda d: d_copy(d, me_v).start())
    own_gram = dot_t(positions, deviation, lax.Precision.HIGHEST)

    live = count_ref[0]

    def is_live(s):
        return jnp.minimum(jnp.maximum(live - s, 0), 1)

    each(1, views, lambda d: x_copy(d, origin(d)).wait_recv())
    for c in range(CHUNKS):
        tile_copy(c).wait()

    def forward_group(first):
        lefts, rights = [], []
        for k in range(GROUP):
            s = first + k
            start = is_live(s) * (ray_blocks - rays_ref[s])
            window = xpad[voxels_ref[s], pl.ds(start, ray_blocks)]
            lefts.append(window.reshape(ray_blocks * rows, tile))
            rights.append(tiles[s])
        return dot_t(jnp.concatenate(lefts, axis=1), jnp.concatenate(rights, axis=1))

    def adjoint_group(first):
        lefts = []
        for k in range(GROUP):
            s = first + k
            start = is_live(s) * (views - voxels_ref[s])
            window = rpad[rays_ref[s], pl.ds(start, views)]
            lefts.append(window.reshape(views * rows, tile))
        right = tiles[pl.ds(first, GROUP)].reshape(GROUP * tile, tile)
        return jnp.dot(
            jnp.concatenate(lefts, axis=1), right, preferred_element_type=jnp.float32
        )

    def total(group, window, store):
        if window * rows <= 512:
            value = group(0)
            for first in range(GROUP, slots, GROUP):
                value = value + group(first)
            store[...] = value.reshape(store.shape)
        else:
            store[...] = jnp.zeros_like(store)

            @pl.loop(0, slots // GROUP)
            def _(g):
                store[...] += group(g * GROUP).reshape(store.shape)

    total(forward_group, ray_blocks, acc_f)
    for b in range(ray_blocks):
        residual = acc_f[b] - measured_ref[pl.ds(b, 1), :]
        rpad[b, views] = residual.astype(jnp.bfloat16)
    total(adjoint_group, views, back)

    each(1, views, lambda d: b_copy(d, lax.rem(me_v + d, views), me_v).start())
    brecv[me_v] = back[me_v]

    each(1, views, lambda d: d_copy(d, origin(d)).wait_recv())
    if views <= 16:
        wide = jnp.concatenate([back[v] for v in range(views)], axis=1)
        spread = jnp.concatenate([devs[v] for v in range(views)], axis=1)
        high, low = split_high_low(wide)
        gram = dot_t(high, spread) + dot_t(low, spread)
    else:

        def add(v, gram):
            high, low = split_high_low(back[v])
            return gram + dot_t(high, devs[v]) + dot_t(low, devs[v])

        gram = lax.fori_loop(0, views, add, jnp.zeros((rows, walkers), jnp.float32))
    grecv[me_v] = misfit_weight * gram + own_gram
    each(1, views, lambda d: g_copy(d, me_v).start())

    each(1, views, lambda d: b_copy(d, 0, origin(d)).wait_recv())
    grad_ref[...] = misfit_weight * jnp.sum(brecv[...], axis=0) + positions

    each(1, views, lambda d: g_copy(d, origin(d)).wait_recv())
    gram = jnp.sum(grecv[...], axis=0)
    step_size = walkers / (4.0 * (voxel_count + 1))
    coefficient = (
        -(step_size / walkers) * gram
        + math.sqrt(2.0 * step_size / walkers) * noise_ref[...]
    )
    moved = jnp.dot(
        coefficient,
        deviation,
        precision=lax.Precision.HIGHEST,
        preferred_element_type=jnp.float32,
    )
    own_deviation = positions - mean
    disp_ref[...] = moved + step_size * (voxel_count + 1) / walkers * own_deviation

    each(1, walks, lambda d: w_copy(d, me_w).wait_send())

    def drain(d):
        x_copy(d, me_v).wait_send()
        d_copy(d, me_v).wait_send()
        b_copy(d, 0, me_v).wait_send()
        g_copy(d, me_v).wait_send()

    each(1, views, drain)


def shards(views, walks, positions, tile_values, tile_rays, tile_voxels, tile_count, measured, langevin_noise):
    rows, tile = positions.shape
    slots = tile_values.shape[0]
    ray_blocks = measured.shape[0] // tile
    walkers = rows * walks
    dma = pltpu.SemaphoreType.DMA
    vmem = pl.BlockSpec(memory_space=pltpu.VMEM)
    smem = pl.BlockSpec(memory_space=pltpu.SMEM)
    out = jax.ShapeDtypeStruct((rows, tile), jnp.float32)
    return pl.pallas_call(
        functools.partial(step_kernel, views, walks),
        out_shape=(out, out),
        in_specs=[
            vmem,
            pl.BlockSpec(memory_space=pl.ANY),
            smem,
            smem,
            smem,
            vmem,
            vmem,
        ],
        out_specs=(vmem, vmem),
        scratch_shapes=[
            pltpu.VMEM((slots, tile, tile), jnp.bfloat16),
            pltpu.VMEM((views, 2 * ray_blocks, rows, tile), jnp.bfloat16),
            pltpu.VMEM((ray_blocks, 2 * views, rows, tile), jnp.bfloat16),
            pltpu.VMEM((walks, rows, tile), jnp.float32),
            pltpu.VMEM((views, walkers, tile), jnp.bfloat16),
            pltpu.VMEM((views, rows, tile), jnp.float32),
            pltpu.VMEM((views, rows, tile), jnp.float32),
            pltpu.VMEM((views, rows, walkers), jnp.float32),
            pltpu.VMEM((ray_blocks, rows, tile), jnp.float32),
            dma((CHUNKS,)),
            dma((views,)),
            dma((views,)),
            dma((walks,)),
            dma((walks,)),
            dma((views,)),
            dma((views,)),
            dma((views,)),
            dma((views,)),
            dma((views,)),
            dma((views,)),
        ],
        compiler_params=pltpu.CompilerParams(
            collective_id=0,
            has_side_effects=True,
            vmem_limit_bytes=56 * 1024 * 1024,
        ),
        cost_estimate=pl.CostEstimate(
            flops=4 * slots * tile * tile * rows,
            bytes_accessed=2 * slots * tile * tile,
            transcendentals=0,
        ),
    )(
        positions,
        tile_values,
        tile_rays,
        tile_voxels,
        tile_count,
        measured.reshape(ray_blocks, tile),
        langevin_noise,
    )


def solution(mesh):
    in_specs = (
        P("walk", "view"),
        P("view", None, None),
        P("view"),
        P("view"),
        P("view"),
        P("view"),
        P("walk", None),
    )
    out_specs = (P("walk", "view"), P("walk", "view"))
    body = functools.partial(shards, mesh.shape["view"], mesh.shape["walk"])
    return jax.shard_map(body, mesh=mesh, in_specs=in_specs, out_specs=out_specs, check_vma=False)
```

time: 79.7 us -> 22.7 us (0.28)
  blocking collectives: 36.2 us -> 0 us
  waiting for transfers between devices: 18.5 us -> 0 us
  Pallas kernels: 0 us -> 18.4 us
  between operations: 14.8 us -> 1.29 us
  other arithmetic: 4.22 us -> 0 us
  matrix products: 3.67 us -> 0 us
    all_gather x2 -> x0, blocking collectives: 23.7 us -> none  [the longest x1 13.4 us: shards(): ensemble = lax.all_gather(positions, 'walk', axis=0, tiled=True)]
    reduce_scatter x1 -> x0, waiting for transfers between devices: 18.5 us -> none  [shards(): lax.psum_scatter(partial_back, 'view', scatter_dimension=1, tiled=True)]
    pallas_call x0 -> x1, Pallas kernels: none -> 18.4 us  [shards(): pl.pallas_call(functools.partial(step_kernel, views, walks), out_shape=(o...]
    psum x1 -> x0, blocking collectives: 12.5 us -> none  [shards(): gram_matrix = lax.psum(gram_part, 'view')]
    dot_general x6 -> x0, matrix products: 3.67 us -> none  [the longest x1 1.23 us: kernel(): jnp.einsum('gri,jgi->gjr', values, picked, preferred_element_type=jnp.flo...]
    unnamed x15 -> x2, local copies, waits for them, and re-layouts: 0.68 us -> 2.59 us
    select_n x2 -> x0, other arithmetic: 1.45 us -> none  [the longest x1 0.8 us: kernel(): picked = jnp.take(blocks, vox_ids, axis=1)]
    and x2 -> x0, other arithmetic: 1.32 us -> none  [the longest x1 0.66 us: kernel(): picked = jnp.take(residual_blocks, ray_ids, axis=1)]
  transfers between devices with their start and end apart: 1 -> 0, of which waited for: 1 -> 0; matrix products, arithmetic and copies ran while one was open for 0% -> 0% of each run, Pallas kernels for 0% -> 0%
where the time goes in v1:
time: 22.7 us; the launch traced here: 22.3 us
  Pallas kernels  18.4 us (81%)
  local copies, waits for them, and re-layouts  2.59 us (11%)
  between operations  1.29 us (6%)
    pallas_call x1, Pallas kernels, shards(): pl.pallas_call(functools.partial(step_kernel, views, walks), out_shape=(o...  18.4 us
    unnamed x2, local copies, waits for them, and re-layouts  2.59 us

profile of v1, /device:TPU:0, one launch (start us, length us, event | category | flops | bytes accessed | tf_op | source)
XLA Modules:
  0.0 22.3 jit_solution(13441786501596557621)
XLA Ops:
  1.3 18.4 %shard_map.86 = (f32[16,128]{1,0:T(8,128)}, f32[16,128]{1,0:T(8,128)}) custom-call(f32[16,128]{1,0:T(8,128)} %pos_ref.1, bf16[64,128,128]{2,1,0:T(8,128)(2,1)} %tiles_hbm.1, s32[64]{0:T(128)} %rays_ref.1, s32[64]{0:T(128)} %voxels_ref.1, s32[1]{0:T(128)S(6)} %copy.11.count_ref, f32[16,128]{1,0:T(8,128)} %bitcast.1, f32[16,64]{1,0:T(8,128)} %noise_ref.1), custom_call_target="tpu_custom_call" | custom-call | flops 67108864 | bytes 2097152 | tf_op jit(solution)/shard_map/pallas_call | solution.py:284
  19.7 1.3 %copy.12 = f32[16,128]{1,0:T(8,128)} copy(f32[16,128]{1,0:T(8,128)} %get-tuple-element.4) | data formatting | bytes 16384
  21.0 1.3 %copy.13 = f32[16,128]{1,0:T(8,128)} copy(f32[16,128]{1,0:T(8,128)} %get-tuple-element.5) | data formatting | bytes 16384

commit v2 on v1

--- a/solution.py
+++ b/solution.py
@@ -46,13 +46,19 @@
     walks,
     pos_ref,
     tiles_hbm,
+    rays_hbm,
+    voxels_hbm,
+    count_hbm,
+    measured_hbm,
+    noise_hbm,
+    grad_ref,
+    disp_ref,
     rays_ref,
     voxels_ref,
     count_ref,
     measured_ref,
     noise_ref,
-    grad_ref,
-    disp_ref,
+    small_sem,
     tiles,
     xpad,
     rpad,
@@ -108,6 +114,20 @@
         part = pl.ds(c * chunk, chunk)
         return pltpu.make_async_copy(tiles_hbm.at[part], tiles.at[part], tile_sem.at[c])
 
+    small = [
+        pltpu.make_async_copy(source, target, small_sem.at[k])
+        for k, (source, target) in enumerate(
+            (
+                (rays_hbm, rays_ref),
+                (voxels_hbm, voxels_ref),
+                (count_hbm, count_ref),
+                (measured_hbm, measured_ref),
+                (noise_hbm, noise_ref),
+            )
+        )
+    ]
+    for copy in small:
+        copy.start()
     for c in range(CHUNKS):
         tile_copy(c).start()
 
@@ -173,6 +193,8 @@
     each(1, views, lambda d: d_copy(d, me_v).start())
     own_gram = dot_t(positions, deviation, lax.Precision.HIGHEST)
 
+    for copy in small:
+        copy.wait()
     live = count_ref[0]
 
     def is_live(s):
@@ -279,22 +301,20 @@
     walkers = rows * walks
     dma = pltpu.SemaphoreType.DMA
     vmem = pl.BlockSpec(memory_space=pltpu.VMEM)
-    smem = pl.BlockSpec(memory_space=pltpu.SMEM)
-    out = jax.ShapeDtypeStruct((rows, tile), jnp.float32)
-    return pl.pallas_call(
+    hbm = pl.BlockSpec(memory_space=pltpu.HBM)
+    held = pltpu.VMEM((rows, tile), jnp.float32)
+    gradient, displacement = pl.pallas_call(
         functools.partial(step_kernel, views, walks),
-        out_shape=(out, out),
-        in_specs=[
-            vmem,
-            pl.BlockSpec(memory_space=pl.ANY),
-            smem,
-            smem,
-            smem,
-            vmem,
-            vmem,
-        ],
+        out_shape=(held, held),
+        in_specs=[vmem, hbm, hbm, hbm, hbm, hbm, hbm],
         out_specs=(vmem, vmem),
         scratch_shapes=[
+            pltpu.SMEM(tile_rays.shape, jnp.int32),
+            pltpu.SMEM(tile_voxels.shape, jnp.int32),
+            pltpu.SMEM(tile_count.shape, jnp.int32),
+            pltpu.VMEM((ray_blocks, tile), jnp.float32),
+            pltpu.VMEM(langevin_noise.shape, jnp.float32),
+            dma((5,)),
             pltpu.VMEM((slots, tile, tile), jnp.bfloat16),
             pltpu.VMEM((views, 2 * ray_blocks, rows, tile), jnp.bfloat16),
             pltpu.VMEM((ray_blocks, 2 * views, rows, tile), jnp.bfloat16),
@@ -335,6 +355,7 @@
         measured.reshape(ray_blocks, tile),
         langevin_noise,
     )
+    return gradient, displacement
 
 
 def solution(mesh):

time: 22.7 us -> 20.4 us (0.90)
  local copies, waits for them, and re-layouts: 2.59 us -> 1.2 us
  Pallas kernels: 18.4 us -> 17.7 us
    unnamed x2, local copies, waits for them, and re-layouts: 2.59 us -> 1.2 us
    pallas_call x1, Pallas kernels: 18.4 us -> 17.7 us  [shards(): pl.pallas_call(functools.partial(step_kernel, views, walks), out_shape=(h...]
where the time goes in v2:
time: 20.4 us; the launch traced here: 20.2 us
  Pallas kernels  17.7 us (87%)
  between operations  1.29 us (6%)
  local copies, waits for them, and re-layouts  1.2 us (6%)
    pallas_call x1, Pallas kernels, shards(): pl.pallas_call(functools.partial(step_kernel, views, walks), out_shape=(h...  17.7 us
    unnamed x2, local copies, waits for them, and re-layouts  1.2 us

profile of v2, /device:TPU:0, one launch (start us, length us, event | category | flops | bytes accessed | tf_op | source)
XLA Modules:
  0.0 20.2 jit_solution(4691256008767058056)
XLA Ops:
  1.3 17.7 %shard_map.86 = (f32[16,128]{1,0:T(8,128)S(1)}, f32[16,128]{1,0:T(8,128)S(1)}) custom-call(f32[16,128]{1,0:T(8,128)} %pos_ref.1, bf16[64,128,128]{2,1,0:T(8,128)(2,1)} %tiles_hbm.1, s32[64]{0:T(128)} %rays_hbm.1, s32[64]{0:T(128)} %voxels_hbm.1, s32[1]{0:T(128)S(6)} %copy.13.count_hbm, f32[16,128]{1,0:T(8,128)} %bitcast.1, f32[16,64]{1,0:T(8,128)} %noise_hbm.1), custom_call_target="tpu_custom_call" | custom-call | flops 67108864 | bytes 2097152 | tf_op jit(solution)/shard_map/pallas_call | solution.py:306
  19.0 0.6 %copy.11 = f32[16,128]{1,0:T(8,128)} copy(f32[16,128]{1,0:T(8,128)S(1)} %get-tuple-element.2) | data formatting | bytes 16384
  19.6 0.6 %copy.12 = f32[16,128]{1,0:T(8,128)} copy(f32[16,128]{1,0:T(8,128)S(1)} %get-tuple-element.3) | data formatting | bytes 16384

commit v3 on v2

--- a/solution.py
+++ b/solution.py
@@ -51,8 +51,7 @@
     count_hbm,
     measured_hbm,
     noise_hbm,
-    grad_ref,
-    disp_ref,
+    out_ref,
     rays_ref,
     voxels_ref,
     count_ref,
@@ -173,8 +172,8 @@
     def g_copy(d, owner):
         return view_copy(d, grecv.at[owner], grecv.at[owner], g_send, g_recv)
 
+    each(1, walks, lambda d: w_copy(d, me_w).start())
     each(1, views, lambda d: x_copy(d, me_v).start())
-    each(1, walks, lambda d: w_copy(d, me_w).start())
 
     def clear(ref, index, middle):
         size = ref.shape[1]
@@ -191,7 +190,6 @@
     deviation = ensemble - mean
     devs[me_v] = deviation.astype(jnp.bfloat16)
     each(1, views, lambda d: d_copy(d, me_v).start())
-    own_gram = dot_t(positions, deviation, lax.Precision.HIGHEST)
 
     for copy in small:
         copy.wait()
@@ -247,6 +245,7 @@
 
     each(1, views, lambda d: b_copy(d, lax.rem(me_v + d, views), me_v).start())
     brecv[me_v] = back[me_v]
+    own_gram = dot_t(positions, deviation, lax.Precision.HIGHEST)
 
     each(1, views, lambda d: d_copy(d, origin(d)).wait_recv())
     if views <= 16:
@@ -264,8 +263,16 @@
     grecv[me_v] = misfit_weight * gram + own_gram
     each(1, views, lambda d: g_copy(d, me_v).start())
 
+    def drain(d):
+        x_copy(d, me_v).wait_send()
+        d_copy(d, me_v).wait_send()
+        b_copy(d, 0, me_v).wait_send()
+
+    each(1, walks, lambda d: w_copy(d, me_w).wait_send())
+    each(1, views, drain)
+
     each(1, views, lambda d: b_copy(d, 0, origin(d)).wait_recv())
-    grad_ref[...] = misfit_weight * jnp.sum(brecv[...], axis=0) + positions
+    out_ref[0] = misfit_weight * jnp.sum(brecv[...], axis=0) + positions
 
     each(1, views, lambda d: g_copy(d, origin(d)).wait_recv())
     gram = jnp.sum(grecv[...], axis=0)
@@ -281,17 +288,9 @@
         preferred_element_type=jnp.float32,
     )
     own_deviation = positions - mean
-    disp_ref[...] = moved + step_size * (voxel_count + 1) / walkers * own_deviation
-
-    each(1, walks, lambda d: w_copy(d, me_w).wait_send())
-
-    def drain(d):
-        x_copy(d, me_v).wait_send()
-        d_copy(d, me_v).wait_send()
-        b_copy(d, 0, me_v).wait_send()
-        g_copy(d, me_v).wait_send()
-
-    each(1, views, drain)
+    out_ref[1] = moved + step_size * (voxel_count + 1) / walkers * own_deviation
+
+    each(1, views, lambda d: g_copy(d, me_v).wait_send())
 
 
 def shards(views, walks, positions, tile_values, tile_rays, tile_voxels, tile_count, measured, langevin_noise):
@@ -302,12 +301,11 @@
     dma = pltpu.SemaphoreType.DMA
     vmem = pl.BlockSpec(memory_space=pltpu.VMEM)
     hbm = pl.BlockSpec(memory_space=pltpu.HBM)
-    held = pltpu.VMEM((rows, tile), jnp.float32)
-    gradient, displacement = pl.pallas_call(
+    both = pl.pallas_call(
         functools.partial(step_kernel, views, walks),
-        out_shape=(held, held),
+        out_shape=pltpu.VMEM((2, rows, tile), jnp.float32),
         in_specs=[vmem, hbm, hbm, hbm, hbm, hbm, hbm],
-        out_specs=(vmem, vmem),
+        out_specs=vmem,
         scratch_shapes=[
             pltpu.SMEM(tile_rays.shape, jnp.int32),
             pltpu.SMEM(tile_voxels.shape, jnp.int32),
@@ -355,7 +353,7 @@
         measured.reshape(ray_blocks, tile),
         langevin_noise,
     )
-    return gradient, displacement
+    return both[0], both[1]
 
 
 def solution(mesh):

time: 20.4 us -> 19.8 us (0.971)
  local copies, waits for them, and re-layouts: 1.2 us -> 0.61 us
    unnamed x2 -> x0, local copies, waits for them, and re-layouts: 1.2 us -> none
    squeeze x0 -> x1, local copies, waits for them, and re-layouts: none -> 0.61 us  [shards(): return (both[0], both[1])]
where the time goes in v3:
time: 19.8 us; the launch traced here: 19.5 us
  Pallas kernels  17.6 us (89%)
  between operations  1.29 us (7%)
  local copies, waits for them, and re-layouts  0.61 us (3%)
    pallas_call x1, Pallas kernels, shards(): pl.pallas_call(functools.partial(step_kernel, views, walks), out_shape=pl...  17.6 us
    squeeze x1, local copies, waits for them, and re-layouts, shards(): return (both[0], both[1])  0.61 us

profile of v3, /device:TPU:0, one launch (start us, length us, event | category | flops | bytes accessed | tf_op | source)
XLA Modules:
  0.0 19.5 jit_solution(10809543423129511231)
XLA Ops:
  1.3 17.6 %shard_map.86 = f32[2,16,128]{2,1,0:T(8,128)S(1)} custom-call(f32[16,128]{1,0:T(8,128)} %pos_ref.1, bf16[64,128,128]{2,1,0:T(8,128)(2,1)} %tiles_hbm.1, s32[64]{0:T(128)} %rays_hbm.1, s32[64]{0:T(128)} %voxels_hbm.1, s32[1]{0:T(128)S(6)} %copy.9.count_hbm, f32[16,128]{1,0:T(8,128)} %bitcast.5, f32[16,64]{1,0:T(8,128)} %noise_hbm.1), custom_call_target="tpu_custom_call" | custom-call | flops 67108864 | bytes 2097152 | tf_op jit(solution)/shard_map/pallas_call | solution.py:304
  18.9 0.6 %slice_bitcast_fusion = (f32[16,128]{1,0:T(8,128)}, f32[16,128]{1,0:T(8,128)}) fusion(f32[2,16,128]{2,1,0:T(8,128)S(1)} %shard_map.86), kind=kLoop, calls=%fused_computation | loop fusion | bytes 32768 | tf_op jit(solution)/shard_map/squeeze | solution.py:356

commit v4 on v3

--- a/solution.py
+++ b/solution.py
@@ -140,14 +140,11 @@
         return pltpu.make_async_remote_copy(
             src_ref=src,
             dst_ref=dst,
-            send_sem=send.at[d],
-            recv_sem=recv.at[d],
+            send_sem=send,
+            recv_sem=recv,
             device_id={"view": lax.rem(me_v + d, views)},
             device_id_type=MESH,
         )
-
-    def origin(d):
-        return lax.rem(me_v - d + views, views)
 
     def x_copy(d, owner):
         part = xpad.at[owner, ray_blocks]
@@ -157,8 +154,8 @@
         return pltpu.make_async_remote_copy(
             src_ref=ens.at[owner],
             dst_ref=ens.at[owner],
-            send_sem=w_send.at[d],
-            recv_sem=w_recv.at[d],
+            send_sem=w_send,
+            recv_sem=w_recv,
             device_id={"walk": lax.rem(me_w + d, walks)},
             device_id_type=MESH,
         )
@@ -171,6 +168,24 @@
 
     def g_copy(d, owner):
         return view_copy(d, grecv.at[owner], grecv.at[owner], g_send, g_recv)
+
+    def all_views(like, send, recv):
+        return view_copy(1, like, like, send, recv)
+
+    peers = pl.ds(0, views - 1)
+    x_all = all_views(rpad.at[0, peers], x_send, x_recv)
+    d_all = all_views(devs.at[peers], d_send, d_recv)
+    b_all = all_views(brecv.at[peers], b_send, b_recv)
+    g_all = all_views(grecv.at[peers], g_send, g_recv)
+    w_part = ens.at[pl.ds(0, walks - 1)]
+    w_all = pltpu.make_async_remote_copy(
+        src_ref=w_part,
+        dst_ref=w_part,
+        send_sem=w_send,
+        recv_sem=w_recv,
+        device_id={"walk": lax.rem(me_w + 1, walks)},
+        device_id_type=MESH,
+    )
 
     each(1, walks, lambda d: w_copy(d, me_w).start())
     each(1, views, lambda d: x_copy(d, me_v).start())
@@ -184,7 +199,7 @@
     each(0, views, lambda v: clear(xpad, v, ray_blocks))
     each(0, ray_blocks, lambda b: clear(rpad, b, views))
 
-    each(1, walks, lambda d: w_copy(d, lax.rem(me_w - d + walks, walks)).wait_recv())
+    w_all.wait_recv()
     ensemble = ens[...].reshape(walkers, tile)
     mean = jnp.sum(ensemble, axis=0, keepdims=True) / walkers
     deviation = ensemble - mean
@@ -198,7 +213,7 @@
     def is_live(s):
         return jnp.minimum(jnp.maximum(live - s, 0), 1)
 
-    each(1, views, lambda d: x_copy(d, origin(d)).wait_recv())
+    x_all.wait_recv()
     for c in range(CHUNKS):
         tile_copy(c).wait()
 
@@ -247,7 +262,7 @@
     brecv[me_v] = back[me_v]
     own_gram = dot_t(positions, deviation, lax.Precision.HIGHEST)
 
-    each(1, views, lambda d: d_copy(d, origin(d)).wait_recv())
+    d_all.wait_recv()
     if views <= 16:
         wide = jnp.concatenate([back[v] for v in range(views)], axis=1)
         spread = jnp.concatenate([devs[v] for v in range(views)], axis=1)
@@ -262,19 +277,13 @@
         gram = lax.fori_loop(0, views, add, jnp.zeros((rows, walkers), jnp.float32))
     grecv[me_v] = misfit_weight * gram + own_gram
     each(1, views, lambda d: g_copy(d, me_v).start())
-
-    def drain(d):
-        x_copy(d, me_v).wait_send()
-        d_copy(d, me_v).wait_send()
-        b_copy(d, 0, me_v).wait_send()
-
-    each(1, walks, lambda d: w_copy(d, me_w).wait_send())
-    each(1, views, drain)
-
-    each(1, views, lambda d: b_copy(d, 0, origin(d)).wait_recv())
+    for sent in (w_all, x_all, d_all, b_all):
+        sent.wait_send()
+
+    b_all.wait_recv()
     out_ref[0] = misfit_weight * jnp.sum(brecv[...], axis=0) + positions
 
-    each(1, views, lambda d: g_copy(d, origin(d)).wait_recv())
+    g_all.wait_recv()
     gram = jnp.sum(grecv[...], axis=0)
     step_size = walkers / (4.0 * (voxel_count + 1))
     coefficient = (
@@ -290,7 +299,7 @@
     own_deviation = positions - mean
     out_ref[1] = moved + step_size * (voxel_count + 1) / walkers * own_deviation
 
-    each(1, views, lambda d: g_copy(d, me_v).wait_send())
+    g_all.wait_send()
 
 
 def shards(views, walks, positions, tile_values, tile_rays, tile_voxels, tile_count, measured, langevin_noise):
@@ -323,16 +332,16 @@
             pltpu.VMEM((views, rows, walkers), jnp.float32),
             pltpu.VMEM((ray_blocks, rows, tile), jnp.float32),
             dma((CHUNKS,)),
-            dma((views,)),
-            dma((views,)),
-            dma((walks,)),
-            dma((walks,)),
-            dma((views,)),
-            dma((views,)),
-            dma((views,)),
-            dma((views,)),
-            dma((views,)),
-            dma((views,)),
+            dma,
+            dma,
+            dma,
+            dma,
+            dma,
+            dma,
+            dma,
+            dma,
+            dma,
+            dma,
         ],
         compiler_params=pltpu.CompilerParams(
             collective_id=0,

time: 19.8 us -> 19.2 us (0.970)
  Pallas kernels: 17.6 us -> 17.1 us
    pallas_call x1, Pallas kernels: 17.6 us -> 17.1 us  [shards(): pl.pallas_call(functools.partial(step_kernel, views, walks), out_shape=pl...]
where the time goes in v4:
time: 19.2 us; the launch traced here: 19 us
  Pallas kernels  17.1 us (89%)
  between operations  1.29 us (7%)
  local copies, waits for them, and re-layouts  0.61 us (3%)
    pallas_call x1, Pallas kernels, shards(): pl.pallas_call(functools.partial(step_kernel, views, walks), out_shape=pl...  17.1 us
    squeeze x1, local copies, waits for them, and re-layouts, shards(): return (both[0], both[1])  0.61 us

profile of v4, /device:TPU:0, one launch (start us, length us, event | category | flops | bytes accessed | tf_op | source)
XLA Modules:
  0.0 19.0 jit_solution(4097523590869776532)
XLA Ops:
  1.3 17.1 %shard_map.86 = f32[2,16,128]{2,1,0:T(8,128)S(1)} custom-call(f32[16,128]{1,0:T(8,128)} %pos_ref.1, bf16[64,128,128]{2,1,0:T(8,128)(2,1)} %tiles_hbm.1, s32[64]{0:T(128)} %rays_hbm.1, s32[64]{0:T(128)} %voxels_hbm.1, s32[1]{0:T(128)S(6)} %copy.9.count_hbm, f32[16,128]{1,0:T(8,128)} %bitcast.5, f32[16,64]{1,0:T(8,128)} %noise_hbm.1), custom_call_target="tpu_custom_call" | custom-call | flops 67108864 | bytes 2097152 | tf_op jit(solution)/shard_map/pallas_call | solution.py:313
  18.4 0.6 %slice_bitcast_fusion = (f32[16,128]{1,0:T(8,128)}, f32[16,128]{1,0:T(8,128)}) fusion(f32[2,16,128]{2,1,0:T(8,128)S(1)} %shard_map.86), kind=kLoop, calls=%fused_computation | loop fusion | bytes 32768 | tf_op jit(solution)/shard_map/squeeze | solution.py:365

commit v5 on v4

--- a/solution.py
+++ b/solution.py
@@ -11,7 +11,7 @@
 misfit_weight = 4.0
 MESH = pl.DeviceIdType.MESH
 GROUP = 8
-CHUNKS = 4
+CHUNKS = 1
 
 
 def each(start, stop, body):
@@ -125,10 +125,6 @@
             )
         )
     ]
-    for copy in small:
-        copy.start()
-    for c in range(CHUNKS):
-        tile_copy(c).start()
 
     positions = pos_ref[...]
     xpad[me_v, ray_blocks] = positions.astype(jnp.bfloat16)
@@ -189,6 +185,10 @@
 
     each(1, walks, lambda d: w_copy(d, me_w).start())
     each(1, views, lambda d: x_copy(d, me_v).start())
+    for copy in small:
+        copy.start()
+    for c in range(CHUNKS):
+        tile_copy(c).start()
 
     def clear(ref, index, middle):
         size = ref.shape[1]

time: 19.2 us -> 19.2 us (level)
  no operation moved by 1% of the time
where the time goes in v5:
time: 19.2 us; the launch traced here: 18.9 us
  Pallas kernels  17 us (89%)
  between operations  1.29 us (7%)
  local copies, waits for them, and re-layouts  0.61 us (3%)
    pallas_call x1, Pallas kernels, shards(): pl.pallas_call(functools.partial(step_kernel, views, walks), out_shape=pl...  17 us
    squeeze x1, local copies, waits for them, and re-layouts, shards(): return (both[0], both[1])  0.61 us

profile of v5, /device:TPU:0, one launch (start us, length us, event | category | flops | bytes accessed | tf_op | source)
XLA Modules:
  0.0 18.9 jit_solution(16634757294400298933)
XLA Ops:
  1.3 17.0 %shard_map.86 = f32[2,16,128]{2,1,0:T(8,128)S(1)} custom-call(f32[16,128]{1,0:T(8,128)} %pos_ref.1, bf16[64,128,128]{2,1,0:T(8,128)(2,1)} %tiles_hbm.1, s32[64]{0:T(128)} %rays_hbm.1, s32[64]{0:T(128)} %voxels_hbm.1, s32[1]{0:T(128)S(6)} %copy.9.count_hbm, f32[16,128]{1,0:T(8,128)} %bitcast.5, f32[16,64]{1,0:T(8,128)} %noise_hbm.1), custom_call_target="tpu_custom_call" | custom-call | flops 67108864 | bytes 2097152 | tf_op jit(solution)/shard_map/pallas_call | solution.py:313
  18.3 0.6 %slice_bitcast_fusion = (f32[16,128]{1,0:T(8,128)}, f32[16,128]{1,0:T(8,128)}) fusion(f32[2,16,128]{2,1,0:T(8,128)S(1)} %shard_map.86), kind=kLoop, calls=%fused_computation | loop fusion | bytes 32768 | tf_op jit(solution)/shard_map/squeeze | solution.py:365
